TPU v7x, 32 devices: a whole 2x2x4 slice. The times are simulated.
32 devices in a mesh: dp: 8 (over y, x, core), feat: 4 (over z).
Axes of the slice: x: 2, y: 2, z: 4, core: 2. Of those that a mesh axis runs over, the one named last changes fastest.
Arguments:
- tokens: bfloat16 [8192, 1024], P('dp'), may hold values from -6 to 6
- cotangent: bfloat16 [8192, 1024], P('dp'), may hold values from -6 to 6
- doc_starts: int32 [8, 8], P('dp'), may hold values from 0 to 1023, as said below
- queries_keys: float32 [1024, 512], P(None, 'feat'), may hold values from -0.1875 to 0.1875
- value_weight: float32 [1024, 1024], P(None, 'feat'), may hold values from -0.1875 to 0.1875
- out_weight: float32 [1024, 1024], P('feat'), may hold values from -1 to 1
- gate_up: float32 [2, 1024, 2752], P(None, None, 'feat'), may hold values from -0.1875 to 0.1875
- down_weight: float32 [2752, 1024], P('feat'), may hold values from -0.109375 to 0.109375
- norm_gains: float32 [2, 1024], replicated, may hold values from 0.5 to 1.5
- queries_moment: float32 [1024, 512], P(None, 'feat'), may hold values from -224 to 224
- value_moment: float32 [1024, 1024], P(None, 'feat'), may hold values from -224 to 224
- out_moment: float32 [1024, 1024], P('feat'), may hold values from -224 to 224
- gate_moment: float32 [2, 1024, 2752], P(None, None, 'feat'), may hold values from -224 to 224
- down_moment: float32 [2752, 1024], P('feat'), may hold values from -224 to 224
- gains_moment: float32 [2, 1024], replicated, may hold values from -512 to 512
- queries_average: float32 [1024, 512], P(None, 'feat'), may hold values from -0.1875 to 0.1875
- value_average: float32 [1024, 1024], P(None, 'feat'), may hold values from -0.1875 to 0.1875
- out_average: float32 [1024, 1024], P('feat'), may hold values from -1 to 1
- gate_average: float32 [2, 1024, 2752], P(None, None, 'feat'), may hold values from -0.1875 to 0.1875
- down_average: float32 [2752, 1024], P('feat'), may hold values from -0.109375 to 0.109375
- gains_average: float32 [2, 1024], replicated, may hold values from 0.5 to 1.5
Outputs:
- mixed: bfloat16 [8192, 1024], P('dp')
- input_gradient: float32 [8192, 1024], P('dp')
- queries_momentum: float32 [1024, 512], P(None, 'feat')
- queries_new: float32 [1024, 512], P(None, 'feat')
- queries_mean: float32 [1024, 512], P(None, 'feat')
- value_momentum: float32 [1024, 1024], P(None, 'feat')
- value_new: float32 [1024, 1024], P(None, 'feat')
- value_mean: float32 [1024, 1024], P(None, 'feat')
- out_momentum: float32 [1024, 1024], P('feat')
- out_new: float32 [1024, 1024], P('feat')
- out_mean: float32 [1024, 1024], P('feat')
- gate_momentum: float32 [2, 1024, 2752], P(None, None, 'feat')
- gate_new: float32 [2, 1024, 2752], P(None, None, 'feat')
- gate_mean: float32 [2, 1024, 2752], P(None, None, 'feat')
- down_momentum: float32 [2752, 1024], P('feat')
- down_new: float32 [2752, 1024], P('feat')
- down_mean: float32 [2752, 1024], P('feat')
- gains_momentum: float32 [2, 1024], replicated
- gains_new: float32 [2, 1024], replicated
- gains_mean: float32 [2, 1024], replicated
Inputs may be any that keep to these rules, and one draw needn't show every extreme that they name: `doc_starts`: each row's first start is 0, its last is 1023, and its 8 starts strictly increase.
All inputs are finite; a program needn't handle non-finite values.
Results may differ from a plain program's by a relative error of at most 0.015.
Values may be sent and summed in bfloat16 or wider, within the bound.
A program may use at most 256 MiB of HBM per device.

v0:
```python
import functools
import jax
import jax.numpy as jnp
from jax import lax
from jax.experimental import pallas as pl
from jax.experimental.pallas import tpu as pltpu
from jax.sharding import PartitionSpec as P

D = 1024
HEADS = 16
QK = 16
HV = 64
FF = 2752
STEP = 4
BT = 256
F32 = jnp.float32
BF16 = jnp.bfloat16

MESH = pl.DeviceIdType.MESH
EPS = 1e-06
MOMENTUM = 0.9


def nt(a, b):
    return lax.dot_general(a, b, (((1,), (1,)), ((), ())), preferred_element_type=F32)


def nn(a, b):
    return lax.dot_general(a, b, (((1,), (0,)), ((), ())), preferred_element_type=F32)


class LineSum:
    def __init__(self, part, leaf, mid, total, send, recv, rows, lags=(0, 2, 4)):
        self.part, self.leaf, self.mid, self.total, self.send, self.recv = part, leaf, mid, total, send, recv
        self.rows, self.lags = rows, lags
        self.count = part.shape[0] // rows
        self.dp, self.f = lax.axis_index("dp"), lax.axis_index("feat")

    def place(self, c):
        odd = lax.rem(c, 2)
        return self.f + odd * (3 - 2 * self.f), 1 - 2 * odd

    def copy(self, c, src, dst, kind, slot, to):
        at = pl.ds(pl.multiple_of(c * self.rows, self.rows), self.rows)
        return pltpu.make_async_remote_copy(
            src_ref=src.at[at], dst_ref=dst.at[at], send_sem=self.send.at[slot], recv_sem=self.recv.at[min(kind, 1), c],
            device_id=(self.dp, to), device_id_type=MESH)

    def leaves(self, c):
        p, up = self.place(c)

        @pl.when(p == 3)
        def _():
            self.copy(c, self.part, self.leaf, 0, 0, self.f - up).start()

        @pl.when(p == 0)
        def _():
            self.copy(c, self.part, self.leaf, 0, 0, self.f + up).start()

    def middle(self, c):
        p, up = self.place(c)
        at = pl.ds(pl.multiple_of(c * self.rows, self.rows), self.rows)

        @pl.when(p == 2)
        def _():
            self.copy(c, self.part, self.leaf, 0, 0, self.f).wait_recv()
            self.part[at, :] = self.part[at, :] + self.leaf[at, :]
            self.copy(c, self.part, self.mid, 1, 0, self.f - up).start()

    def root(self, c):
        p, up = self.place(c)
        at = pl.ds(pl.multiple_of(c * self.rows, self.rows), self.rows)

        @pl.when(p == 1)
        def _():
            self.copy(c, self.part, self.leaf, 0, 0, self.f).wait_recv()
            self.copy(c, self.part, self.mid, 1, 0, self.f).wait_recv()
            self.total[at, :] = self.part[at, :] + self.leaf[at, :] + self.mid[at, :]
            self.copy(c, self.total, self.total, 2, 1, self.f + up).start()
            self.copy(c, self.total, self.total, 2, 0, self.f - up).start()

    def onward(self, c):
        p, up = self.place(c)

        @pl.when(p == 2)
        def _():
            self.copy(c, self.total, self.total, 2, 0, self.f).wait_recv()
            self.copy(c, self.total, self.total, 2, 1, self.f + up).start()

    def serve(self, i):
        for lag, act in zip(self.lags, (self.middle, self.root, self.onward)):
            c = i - lag

            @pl.when(jnp.logical_and(c >= 0, c < self.count))
            def _():
                act(c)

    def steps(self):
        return self.count + self.lags[-1]

    def arrived(self, c):
        p, up = self.place(c)

        @pl.when(jnp.logical_or(p == 0, p == 3))
        def _():
            self.copy(c, self.total, self.total, 2, 0, self.f).wait_recv()

    def drain(self):
        def all_sent(slot):
            pltpu.make_async_remote_copy(
                src_ref=self.part, dst_ref=self.part, send_sem=self.send.at[slot], recv_sem=self.recv.at[0, 0],
                device_id=(self.dp, self.f), device_id_type=MESH,
            ).wait_send()

        all_sent(0)

        @pl.when(jnp.logical_or(self.f == 1, self.f == 2))
        def _():
            all_sent(1)


class CubeSum:
    def __init__(self, work, recv, out, send_sem, recv_sem, pieces, bits):
        self.work, self.recv, self.out, self.send_sem, self.recv_sem = work, recv, out, send_sem, recv_sem
        self.pieces, self.nb = pieces, len(bits)
        self.dp, self.f = lax.axis_index("dp"), lax.axis_index("feat")
        self.orders = [list(bits), [bits[0]] + list(bits[1:])[::-1]]
        self.bits = bits

    def partner(self, bit):
        return self.dp + bit - 2 * bit * lax.rem(self.dp // bit, 2)

    def lanes(self, colour):
        half = self.work.shape[1] // 2
        return pl.ds(colour * half, half)

    def segment(self, piece, colour, k):
        first, rows = self.pieces[piece]
        start = first
        for bit in self.orders[colour][:k]:
            rows = rows // 2
            start = start + rows * lax.rem(self.dp // bit, 2)
        return start, rows

    def at(self, start, rows):
        return pl.ds(pl.multiple_of(start, 16), rows)

    def halve(self, piece, colour, k):
        start, rows = self.segment(piece, colour, k)
        rows = rows // 2
        bit = self.orders[colour][k]
        own = lax.rem(self.dp // bit, 2)
        first, whole = self.pieces[piece]
        landing = first + whole - 2 * rows
        return pltpu.make_async_remote_copy(
            src_ref=self.work.at[self.at(start + rows * (1 - own), rows), self.lanes(colour)],
            dst_ref=self.recv.at[self.at(landing, rows), self.lanes(colour)],
            send_sem=self.send_sem.at[0], recv_sem=self.recv_sem.at[piece, colour, k],
            device_id=(self.partner(bit), self.f), device_id_type=MESH)

    def add(self, piece, colour, k):
        start, rows = self.segment(piece, colour, k + 1)
        first, whole = self.pieces[piece]
        landing = first + whole - 2 * rows
        target = self.out if k + 1 == self.nb else self.work
        mine = self.work[self.at(start, rows), self.lanes(colour)]
        target[self.at(start, rows), self.lanes(colour)] = mine + self.recv[self.at(landing, rows), self.lanes(colour)]

    def double(self, piece, colour, k):
        start, rows = self.segment(piece, colour, k + 1)
        bit = self.orders[colour][k]
        at = self.at(start, rows)
        slot = 2 * self.nb - 1 - k
        return pltpu.make_async_remote_copy(
            src_ref=self.out.at[at, self.lanes(colour)], dst_ref=self.out.at[at, self.lanes(colour)],
            send_sem=self.send_sem.at[1], recv_sem=self.recv_sem.at[piece, colour, slot],
            device_id=(self.partner(bit), self.f), device_id_type=MESH)

    def launch(self, piece):
        for colour in range(2):
            self.halve(piece, colour, 0).start()

    def advance(self, piece, t):
        for colour in range(2):
            if t < self.nb:
                self.halve(piece, colour, t).wait_recv()
                self.add(piece, colour, t)
                if t + 1 < self.nb:
                    self.halve(piece, colour, t + 1).start()
                else:
                    self.double(piece, colour, self.nb - 1).start()
            else:
                k = 2 * self.nb - 1 - t
                self.double(piece, colour, k).wait_recv()
                if k > 0:
                    self.double(piece, colour, k - 1).start()

    def drain(self):
        rows = self.work.shape[0]
        sent = pl.ds(0, rows - rows // 2**self.nb)
        for n, ref in enumerate((self.work, self.out)):
            pltpu.make_async_remote_copy(
                src_ref=ref.at[sent], dst_ref=ref.at[sent], send_sem=self.send_sem.at[n], recv_sem=self.recv_sem.at[0, 0, 0],
                device_id=(self.dp, self.f), device_id_type=MESH,
            ).wait_send()


def split_rows(rows, unit, count):
    units = rows // unit
    out, first = [], 0
    for n in range(count):
        take = (units * (n + 1) // count - units * n // count) * unit
        out.append((first, take))
        first += take
    return [p for p in out if p[1]]


def own_column(ref, f, width):
    return ref[:, pl.ds(pl.multiple_of(f * width, width), width)]


def greet(line, cube):
    sem = pltpu.get_barrier_semaphore()
    f = lax.axis_index("feat")
    count = jnp.int32(0)
    if cube is not None:
        for bit in cube.bits:
            pl.semaphore_signal(sem, inc=1, device_id=(cube.partner(bit), f), device_id_type=MESH)
        count = count + len(cube.bits)
    if line is not None:
        @pl.when(f > 0)
        def _():
            pl.semaphore_signal(sem, inc=1, device_id=(line.dp, f - 1), device_id_type=MESH)

        @pl.when(f < 3)
        def _():
            pl.semaphore_signal(sem, inc=1, device_id=(line.dp, f + 1), device_id_type=MESH)
        count = count + jnp.where(f > 0, 1, 0) + jnp.where(f < 3, 1, 0)
    pl.semaphore_wait(sem, count)


def each(act, n):
    def body(c, carry):
        act(c)
        return carry

    lax.fori_loop(0, n, body, 0)


def cube_shape(rows, dp_size, count):
    unit = 16 * dp_size
    padded = (rows + unit - 1) // unit * unit
    bits = tuple(2**n for n in range(dp_size.bit_length() - 1))
    return padded, split_rows(padded, unit, count), bits


class Weaver:
    def __init__(self, now, margin=0.5, cost=0.35):
        self.now, self.margin, self.cost = now, margin, cost
        self.streams = {}

    def add(self, name, floors, leads):
        self.streams[name] = [list(floors), list(leads), 0, self.now]

    def ready(self, name):
        floors, leads, n, last = self.streams[name]
        return max(floors[n], last + leads[n])

    def open(self):
        return [name for name, s in self.streams.items() if s[2] < len(s[0])]

    def take(self, name):
        stream = self.streams[name]
        self.now = max(self.now, self.ready(name)) + self.cost
        stream[2] += 1
        stream[3] = self.now
        return name, stream[2] - 1

    def unit(self, length):
        self.now += length
        out = []
        while self.open():
            name = min(self.open(), key=self.ready)
            if self.ready(name) > self.now - self.margin:
                break
            out.append(self.take(name))
        return out

    def until(self, names):
        out = []
        while any(name in names for name in self.open()):
            out.append(self.take(min(self.open(), key=self.ready)))
        return out


def line_floors(line, start):
    pace = line.rows * line.part.shape[1] * 2 / 40e3
    return [start + pace * (n + 1) + 3.0 for n in range(line.steps())]


def cube_floors(cube, start, lag=3.0):
    count = 2 * cube.nb
    ends, floors, times = [start] * len(cube.pieces), [[] for _ in cube.pieces], [[] for _ in cube.pieces]
    for t in range(count):
        near = t in (0, count - 1)
        share = 2 ** (min(t, count - 1 - t) + 1)
        busy = max(ends) if t not in (0, 1, count - 1) else start
        for p, (_, rows) in enumerate(cube.pieces):
            size = rows / share * 1024
            own = 2 * size / 430e3 if near else size / 30e3
            begin = ends[p] + (lag + 0.3 if t else 0.0)
            busy = max(busy, begin) + own
            ends[p] = busy
            floors[p].append(busy + lag)
            times[p].append(own + lag)
    return floors, times


def front_kernel(
    bits, starts_ref, tokens_in, gains_ref, pair_ref, value_ref, out_ref, gate_in, down_in,
    normed_out, pairs_out, values_out, wide_out, gate_out, down_out, attn_out, recip_out, mask_out,
    thin_ref, thick_ref, turned_ref, tokens_ref, gate_f32, down_f32,
    normed_ref, pairs_ref, values_ref, wide_ref, gate_ref, down_ref, attn_ref, recip_ref, mask_ref, acc_ref,
    send_sem, recv_sem, load_sem, store_sem,
):
    dp = lax.axis_index("dp")
    f = lax.axis_index("feat")
    slices = lax.axis_size("feat")
    last = 3
    pieces = 2 ** len(bits)
    j = lax.rem(dp, pieces)
    base = dp - j
    pair_cols, value_cols = pair_ref.shape[1], value_ref.shape[1]
    pairs_wide, values_wide = slices * pair_cols, slices * value_cols
    rows = pair_ref.shape[0] // pieces
    length = tokens_ref.shape[0]
    blocks = length // BT
    loads = [
        pltpu.make_async_copy(a, b, load_sem.at[n])
        for n, (a, b) in enumerate([(tokens_in, tokens_ref), (gate_in, gate_f32), (down_in, down_f32)])
    ]
    loads[0].start()

    def flip(k, bit):
        return k + bit - 2 * bit * lax.rem(k // bit, 2)

    colour_bits = [list(bits[1:]) + [bits[0]], list(bits[1:])[::-1] + [bits[0]]]

    def place(k, colour):
        return sum(k // bit % 2 * 2**n for n, bit in enumerate(colour_bits[colour]))

    def cast(k):
        at = pl.ds(pl.multiple_of(k * rows, rows), rows)
        pair = pair_ref[at, :].astype(BF16)
        thick = value_ref[at, :].astype(BF16)
        turned = out_ref[:, at].T.astype(BF16)
        for colour in range(2):
            part = slice(colour * rows // 2, (colour + 1) * rows // 2)
            thin_ref[colour, place(k, colour), 0] = pair[part]
            thick_ref[colour, place(k, colour), 0] = thick[part]
            turned_ref[colour, place(k, colour), 0] = turned[part]

    cast(j)
    order = [
        jnp.where(f == 0, 1, f - 1),
        jnp.where(f < 2, 2, jnp.where(f == 2, 3, 1)),
        jnp.where(f < 2, 3, 0),
    ]
    barrier = pltpu.get_barrier_semaphore()
    for bit in bits:
        pl.semaphore_signal(barrier, inc=1, device_id=(base + flip(j, bit), f), device_id_type=MESH)
    for z in order:
        pl.semaphore_signal(barrier, inc=1, device_id=(dp, z), device_id_type=MESH)
    pl.semaphore_wait(barrier, len(bits) + last)

    bufs = (thin_ref, thick_ref, turned_ref)
    here = (dp, f)

    def copy(wave, source, target, colour, kind, device, r=None):
        group = 0 if r is None or wave != 1 else r - 1
        return pltpu.make_async_remote_copy(
            src_ref=source, dst_ref=target, send_sem=send_sem.at[wave], recv_sem=recv_sem.at[wave, colour, kind, group],
            device_id=device, device_id_type=MESH,
        )

    for wave in range(3):
        for z in order:
            for colour in range(2):
                at = bufs[wave].at[colour, place(j, colour)]
                r = lax.rem(f - z + slices, slices)
                copy(wave, at.at[0], at.at[r], colour, 0, (dp, z), r).start()

    def held(wave, k, colour, n, r):
        first = place(k, colour) // 2**n * 2**n
        which = pl.ds(1, last) if r is None else pl.ds(r, 1)
        return bufs[wave].at[colour, pl.ds(first, 2**n), which]

    def start_step(wave, n, r):
        for colour in range(2):
            at = held(wave, j, colour, n, r)
            copy(wave, at, at, colour, 1 + n, (base + flip(j, colour_bits[colour][n]), f), r).start()

    def arrive(wave, a=None):
        r = None if a is None else relative[a]
        for colour in range(2):
            at = held(wave, j, colour, 0, r)
            copy(wave, at, at, colour, 0, here, r).wait_recv()
        start_step(wave, 0, r)

    def step(wave, n, a=None):
        r = None if a is None else relative[a]
        for colour in range(2):
            at = held(wave, flip(j, colour_bits[colour][n]), colour, n, r)
            copy(wave, at, at, colour, 1 + n, here, r).wait_recv()
        if n + 1 < len(bits):
            start_step(wave, n + 1, r)

    relative = [lax.rem(z - f + slices, slices) for z in order]

    def put(wave, r, lanes):
        for k in range(pieces):
            for colour in range(2):
                first = k * rows + colour * rows // 2
                wide_ref[first : first + rows // 2, lanes] = bufs[wave][colour, place(k, colour), r]

    def owner(r):
        return lax.rem(f + r, slices)

    def put_thin(r):
        put(0, r, pl.ds(pl.multiple_of(owner(r) * pair_cols, pair_cols), pair_cols))

    def lanes(first, z):
        return pl.ds(pl.multiple_of(first + z * value_cols, 128), value_cols)

    def store(n, source, target, at=None):
        if at is not None:
            source, target = source.at[:, at], target.at[:, at]
        return pltpu.make_async_copy(source, target, store_sem.at[n])

    def use(r):
        z = owner(r)
        put(1, r, lanes(pairs_wide, z))

        def some(n, carry):
            at = pl.ds(pl.multiple_of(n * BT, BT), BT)
            values_ref[at, lanes(0, z)] = nn(normed_ref[at, :], wide_ref[:, lanes(pairs_wide, z)]).astype(BF16)
            return carry

        lax.fori_loop(0, blocks, some, 0)
        store(5, wide_ref, wide_out, lanes(pairs_wide, z)).start()
        store(6, values_ref, values_out, lanes(0, z)).start()

    def put_turned(r):
        at = lanes(pairs_wide + values_wide, owner(r))
        put(2, r, at)
        store(5, wide_ref, wide_out, at).start()

    def cast_rest(n, carry):
        cast(lax.rem(j + n, pieces))
        return carry

    lax.fori_loop(1, pieces, cast_rest, 0)
    loads[0].wait()
    loads[1].start()
    loads[2].start()

    def norm(n, carry):
        at = pl.ds(pl.multiple_of(n * BT, BT), BT)
        x = tokens_ref[at, :].astype(F32)
        scale = lax.rsqrt(jnp.mean(x * x, axis=1, keepdims=True) + EPS)
        normed_ref[at, :] = (x * scale * gains_ref[0:1, :]).astype(BF16)
        return carry

    lax.fori_loop(0, blocks, norm, 0)
    store(0, normed_ref, normed_out).start()
    put_thin(0)
    arrive(0)
    use(0)
    step(0, 0)

    begin = jnp.zeros((length, 1), jnp.int32)
    position = lax.broadcasted_iota(jnp.int32, (length, 1), 0)
    for n in range(starts_ref.shape[1]):
        begin = jnp.where(starts_ref[0, n] <= position, jnp.maximum(begin, starts_ref[0, n]), begin)
    for n in range(blocks):
        rest = length - n * BT
        s = n * BT + lax.broadcasted_iota(jnp.int32, (rest, BT), 1)
        keep = jnp.logical_and(s <= position[n * BT :], s >= begin[n * BT :])
        mask_ref[n, :rest, :] = keep.astype(F32).astype(BF16)
        if n:
            mask_ref[n, rest:, :] = jnp.zeros((n * BT, BT), BF16)
    store(1, mask_ref, mask_out).start()
    def cast_all(source, target):
        def go(m, carry):
            at = pl.ds(pl.multiple_of(m * 16, 16), 16)
            target[at, :] = source[at, :].astype(BF16)
            return carry

        lax.fori_loop(0, source.shape[0] // 16, go, 0)

    step(0, 1)
    arrive(1, 0)
    arrive(1, 1)
    put_turned(0)
    loads[1].wait()
    loads[2].wait()
    cast_all(gate_f32.at[0], gate_ref.at[0])
    step(0, 2)
    step(1, 0, 0)
    arrive(1, 2)
    step(1, 0, 1)
    for r in range(1, slices):
        put_thin(r)

    half = pairs_wide // 2

    def project_pairs(n, carry):
        at = pl.ds(pl.multiple_of(n * BT, BT), BT)
        pairs = nn(normed_ref[at, :], wide_ref[:, :pairs_wide]).astype(BF16)
        pairs_ref[at, :half] = pairs[:, :half] * jnp.bfloat16(0.25)
        pairs_ref[at, half:] = pairs[:, half:]
        return carry

    lax.fori_loop(0, blocks, project_pairs, 0)
    store(4, pairs_ref, pairs_out).start()
    store(5, wide_ref, wide_out, pl.ds(0, pairs_wide)).start()

    lane = lax.broadcasted_iota(jnp.int32, (1, 128), 1)
    def cast_last():
        cast_all(down_f32, down_ref)
        store(2, gate_ref, gate_out).start()
        store(3, down_ref, down_out).start()

    def put_others():
        for r in range(1, slices):
            put_turned(r)

    def cast_up():
        cast_all(gate_f32.at[1], gate_ref.at[1])

    events = {
        1: [(step, 1, 1, 0), (step, 1, 0, 2), (arrive, 2)],
        2: [(cast_up,), (step, 1, 1, 1), (step, 1, 2, 0), (use, relative[0])],
        3: [(step, 1, 1, 2), (step, 2, 0)],
        4: [(step, 1, 2, 1), (use, relative[1])],
        5: [(cast_last,), (step, 2, 1)],
        6: [(step, 1, 2, 2), (use, relative[2])],
        7: [(step, 2, 2), (put_others,)],
    }

    def unit(n, carry):
        for at, acts in events.items():
            @pl.when(n == at)
            def _():
                for act in acts:
                    act[0](*act[1:])
        a = n // 2
        z = jnp.where(a == 0, f, jnp.where(a == 1, order[0], jnp.where(a == 2, order[1], order[2])))
        pair = 2 * z + lax.rem(n, 2)
        vl = pl.ds(pl.multiple_of(pair * 128, 128), 128)
        ql = pl.ds(pl.multiple_of(pair // 4 * 128, 128), 128)
        kl = pl.ds(pl.multiple_of(half + pair // 4 * 128, 128), 128)
        for block in range(blocks):
            first = block * BT
            below, there = pl.ds(first, length - first), pl.ds(first, BT)
            q, k, v = pairs_ref[below, ql], pairs_ref[there, kl], values_ref[there, vl]
            mask = mask_ref[block, : length - first, :]
            for m in range(2):
                own = lane // QK == lax.rem(2 * pair + m, 8)
                t1 = nt(q, jnp.where(own, k, jnp.zeros_like(k))) + 1.0
                p = (t1 * t1 + 1.0).astype(BF16) * mask
                out = nn(p, jnp.where(lane // HV == m, v, jnp.ones_like(v)))
                if block:
                    acc_ref[m, below, :] += out
                else:
                    acc_ref[m] = out
        one, two = acc_ref[0], acc_ref[1]
        numer = jnp.where(lane < HV, one, two)
        recip = 1.0 / pltpu.roll(jnp.where(lane < HV, two, one), HV, 1)
        attn_ref[:, vl] = (numer * recip).astype(BF16)
        recip_ref[:, vl] = recip
        store(7, attn_ref, attn_out, vl).start()
        store(8, recip_ref, recip_out, vl).start()
        return carry

    lax.fori_loop(0, 2 * slices, unit, 0)
    for wave in range(3):
        at = bufs[wave].at[:, :, pl.ds(0, last)]
        copy(wave, at, at, 0, 0, here).wait_send()
    for n, (source, target) in enumerate([
        (normed_ref, normed_out), (mask_ref, mask_out), (gate_ref, gate_out), (down_ref, down_out), (pairs_ref, pairs_out),
        (wide_ref, wide_out), (values_ref, values_out), (attn_ref, attn_out), (recip_ref, recip_out),
    ]):
        store(n, source, target).wait()


def front(starts, tokens, gains, pair_w, value_w, out_w, gate_turned, down):
    length = tokens.shape[0]
    ff = down.shape[0]
    slices = 4
    pair_cols, value_cols = pair_w.shape[1], value_w.shape[1]
    bits = (1, 2, 4)
    hbm = pl.BlockSpec(memory_space=pl.ANY)
    vmem = pl.BlockSpec(memory_space=pltpu.VMEM)
    shapes = [
        ((length, D), BF16),
        ((length, slices * pair_cols), BF16),
        ((length, slices * value_cols), BF16),
        ((D, slices * (pair_cols + 2 * value_cols)), BF16),
        ((2, ff, D), BF16),
        ((ff, D), BF16),
        ((length, slices * value_cols), BF16),
        ((length, slices * value_cols), F32),
        ((length // BT, length, BT), BF16),
    ]
    return pl.pallas_call(
        functools.partial(front_kernel, bits),
        out_shape=tuple(jax.ShapeDtypeStruct(*s) for s in shapes),
        in_specs=[pl.BlockSpec(memory_space=pltpu.SMEM), hbm] + [vmem] * 4 + [hbm] * 2,
        out_specs=(hbm,) * 9,
        scratch_shapes=[
            pltpu.VMEM((2, 8, slices, D // 16, pair_cols), BF16),
            pltpu.VMEM((2, 8, slices, D // 16, value_cols), BF16),
            pltpu.VMEM((2, 8, slices, D // 16, value_cols), BF16),
            pltpu.VMEM((length, D), BF16),
            pltpu.VMEM((2, ff, D), F32),
            pltpu.VMEM((ff, D), F32),
        ]
        + [pltpu.VMEM(*s) for s in shapes]
        + [
            pltpu.VMEM((2, length, 128), F32),
            pltpu.SemaphoreType.DMA((3,)),
            pltpu.SemaphoreType.DMA((3, 2, 4, 3)),
            pltpu.SemaphoreType.DMA((3,)),
            pltpu.SemaphoreType.DMA((9,)),
        ],
        compiler_params=pltpu.CompilerParams(collective_id=1, has_side_effects=True, vmem_limit_bytes=60 * 2**20),
        name="front",
    )(starts, tokens, gains, pair_w, value_w, out_w, gate_turned, down)


def feed_kernel(
    rows, tokens_in, cot_in, attn_in, recip_in, wide_in, gate_in, down_in, gains_ref,
    hidden_out, grad_hidden_out, gn_out, gnt_out, gd_out, ffn_out, grads_out,
    tokens_ref, cot_ref, attn_ref, out_w, gate_ref, down_ref, recip_ref,
    hidden_ref, scale_ref, normed_ref, product_t, gate_t, up_t, own_t, gain_ref, ga_ref, gn_ref, gnt_ref, gd_ref, ffn_ref, grads_ref,
    part, leaf, mid, total, send, recv, load_sem, store_sem,
):
    f = lax.axis_index("feat")
    line = LineSum(part, leaf, mid, total, send, recv, rows, (0, 3, 6))
    length = tokens_ref.shape[0]
    ff = down_ref.shape[0]
    value_cols = own_t.shape[0]
    blocks = length // BT
    first_out = wide_in.shape[1] - attn_ref.shape[1]
    top, others = pl.ds(0, BT), pl.ds(BT, length - BT)
    pairs = [
        (attn_in.at[top], attn_ref.at[top]), (wide_in.at[:, pl.ds(first_out, attn_ref.shape[1])], out_w),
        (tokens_in.at[top], tokens_ref.at[top]), (gate_in, gate_ref), (cot_in.at[top], cot_ref.at[top]), (down_in, down_ref),
        (attn_in.at[others], attn_ref.at[others]), (tokens_in.at[others], tokens_ref.at[others]),
        (cot_in.at[others], cot_ref.at[others]), (recip_in, recip_ref),
    ]
    loads = [pltpu.make_async_copy(a, b, load_sem.at[n]) for n, (a, b) in enumerate(pairs)]
    for load in loads[:6]:
        load.start()
    greet(line, None)
    for load in loads[:6]:
        load.wait()
    for load in loads[6:]:
        load.start()

    def store(source, target, n):
        at = pl.ds(pl.multiple_of(n * BT, BT), BT)
        return pltpu.make_async_copy(source.at[at], target.at[at], store_sem.at[n])

    def block(b, carry):
        at = pl.ds(pl.multiple_of(b * BT, BT), BT)
        turn = 4 * (b - 1)

        @pl.when(b == 1)
        def _():
            for load in loads[6:9]:
                load.wait()

        hidden = tokens_ref[at, :].astype(F32) + nt(attn_ref[at, :], out_w[...])
        hidden_ref[at, :] = hidden
        store(hidden_ref, hidden_out, b).start()
        scale = lax.rsqrt(jnp.mean(hidden * hidden, axis=1, keepdims=True) + EPS)
        scale_ref[at, :] = jnp.broadcast_to(scale, (BT, 128))
        normed = (hidden * scale * gains_ref[1:2, :]).astype(BF16)
        normed_ref[at, :] = normed
        line.serve(turn)
        gate = nt(normed, gate_ref[0])
        up = nt(normed, gate_ref[1])
        line.serve(turn + 1)
        back = nt(cot_ref[at, :], down_ref[...])
        sig = 1.0 / (1.0 + jnp.exp(-gate))
        active = gate * sig
        slope = sig * (1.0 + gate * (1.0 - sig))
        product = (active * up).astype(BF16)
        grad_gate = (back * up * slope).astype(BF16)
        grad_up = (back * active).astype(BF16)
        line.serve(turn + 2)
        part[at, :] = (nn(grad_gate, gate_ref[0]) + nn(grad_up, gate_ref[1])).astype(BF16)

        def out(c, carry):
            line.leaves(b * (BT // rows) + c)
            return carry

        lax.fori_loop(0, BT // rows, out, 0)
        ffn_ref[at, :] = nn(product, down_ref[...]).astype(BF16)
        product_t[:, at] = product.T
        gate_t[:, at] = grad_gate.T
        up_t[:, at] = grad_up.T
        line.serve(turn + 3)
        return carry

    lax.fori_loop(0, blocks, block, 0)
    served = 4 * (blocks - 1)
    gain_ref[...] = jnp.zeros_like(gain_ref)
    chunks = []
    at = 0
    while at < ff:
        chunks.append((at, min(176, ff - at)))
        at += chunks[-1][1]
    for n, (turned, right) in enumerate([(product_t, cot_ref), (gate_t, normed_ref), (up_t, normed_ref)]):
        for first, size in chunks:
            at = slice(n * ff + first, n * ff + first + size)
            grads_ref[at, :] = nn(turned[first : first + size, :], right[...]).astype(BF16)
            line.serve(jnp.int32(served))
            served += 1
    ffn_store = pltpu.make_async_copy(ffn_ref, ffn_out, store_sem.at[blocks])
    ffn_store.start()
    grads_store = pltpu.make_async_copy(
        grads_ref.at[pl.ds(0, 3 * ff)], grads_out.at[pl.ds(0, 3 * ff)], store_sem.at[blocks + 1]
    )
    grads_store.start()
    own_t[...] = own_column(attn_ref, f, value_cols).T
    loads[-1].wait()
    same = lax.broadcasted_iota(jnp.int32, (128, 128), 0) // HV == lax.broadcasted_iota(jnp.int32, (128, 128), 1) // HV
    negate = jnp.where(same, -1.0, 0.0).astype(BF16)
    size = 4 * rows
    units = length // size

    def out(n, source, target, at=None):
        if at is not None:
            source, target = source.at[at], target.at[at]
        return pltpu.make_async_copy(source, target, store_sem.at[blocks + 2 + n])

    def back_rows(u):
        at = pl.ds(u * size, size)
        for c in range(4):
            line.arrived(jnp.int32(4 * u + c))
        if u * size % BT == 0:
            store(hidden_ref, hidden_out, jnp.int32(u * size // BT)).wait()
        hidden, grad = hidden_ref[at, :], total[at, :].astype(F32)
        scale = scale_ref[at, 0:1]
        unit = hidden * scale
        u_two = grad * gains_ref[1:2, :]
        gh = cot_ref[at, :].astype(F32) + scale * (u_two - unit * jnp.mean(u_two * unit, axis=1, keepdims=True))
        hidden_ref[at, :] = gh
        out(0, hidden_ref, grad_hidden_out, at).start()
        ga_ref[at, :] = gh.astype(BF16)
        gain_ref[0:1, :] += jnp.sum(grad * unit, axis=0, keepdims=True)

    def prepare(u, half):
        at = pl.ds(u * size, size)
        ga = ga_ref[at, :]
        for m in range(2):
            wide = pl.ds((2 * half + m) * 256, 256)
            numer = nn(ga, out_w[:, wide]) * (2.0 * recip_ref[at, wide])
            low = numer.astype(BF16)
            both = (numer * attn_ref[at, wide].astype(F32)).astype(BF16)
            gn_ref[at, wide] = low
            gnt_ref[wide, at] = low.T
            gd_ref[at, wide] = jnp.concatenate([nn(both[:, :128], negate), nn(both[:, 128:], negate)], axis=1).astype(BF16)
        if half:
            out(1, gn_ref, gn_out, at).start()
            out(2, gd_ref, gd_out, at).start()
            out(3, gnt_ref, gnt_out, (slice(None), at)).start()

    tasks = [(u, q) for u in range(units) for q in range(3)]
    while tasks:
        if served < line.steps():
            line.serve(jnp.int32(served))
            served += 1
        for _ in range(2):
            if tasks and (served >= line.steps() or served > 4 * tasks[0][0] + 4 + line.lags[-1] + tasks[0][1]):
                u, q = tasks.pop(0)
                if q == 0:
                    back_rows(u)
                else:
                    prepare(u, q - 1)
    first = 3 * ff
    grads_ref[first : first + value_cols, :] = nn(own_t[...], ga_ref[...]).astype(BF16)
    first = first + value_cols
    rest = grads_ref.shape[0] - first
    grads_ref[first:, :] = jnp.zeros((rest, D), BF16)
    grads_ref[first : first + 16, :] = gain_ref[...].astype(BF16)
    last = pl.ds(3 * ff, grads_ref.shape[0] - 3 * ff)
    last_store = pltpu.make_async_copy(grads_ref.at[last], grads_out.at[last], store_sem.at[blocks + 6])
    last_store.start()
    line.drain()
    out(0, hidden_ref, grad_hidden_out).wait()
    out(1, gn_ref, gn_out).wait()
    out(2, gd_ref, gd_out).wait()
    out(3, gnt_ref, gnt_out).wait()
    ffn_store.wait()
    grads_store.wait()
    last_store.wait()


def feed(tokens, cotangent, attn, recip, wide, gate_turned, down, gains, padded):
    length = tokens.shape[0]
    ff = down.shape[0]
    nv, rows = attn.shape[1], 32
    count = length // rows
    hbm = pl.BlockSpec(memory_space=pl.ANY)
    vmem = pl.BlockSpec(memory_space=pltpu.VMEM)
    return pl.pallas_call(
        functools.partial(feed_kernel, rows),
        out_shape=(
            jax.ShapeDtypeStruct((length, D), F32),
            jax.ShapeDtypeStruct((length, D), F32),
            jax.ShapeDtypeStruct((length, nv), BF16),
            jax.ShapeDtypeStruct((nv, length), BF16),
            jax.ShapeDtypeStruct((length, nv), BF16),
            jax.ShapeDtypeStruct((length, D), BF16),
            jax.ShapeDtypeStruct((padded, D), BF16),
        ),
        in_specs=[hbm] * 7 + [vmem],
        out_specs=(hbm,) * 7,
        scratch_shapes=[
            pltpu.VMEM((length, D), BF16), pltpu.VMEM((length, D), BF16), pltpu.VMEM((length, nv), BF16),
            pltpu.VMEM((D, nv), BF16), pltpu.VMEM((2, ff, D), BF16), pltpu.VMEM((ff, D), BF16), pltpu.VMEM((length, nv), F32),
            pltpu.VMEM((length, D), F32), pltpu.VMEM((length, 128), F32), pltpu.VMEM((length, D), BF16),
            pltpu.VMEM((ff, length), BF16), pltpu.VMEM((ff, length), BF16), pltpu.VMEM((ff, length), BF16),
            pltpu.VMEM((nv // 4, length), BF16), pltpu.VMEM((16, D), F32), pltpu.VMEM((length, D), BF16),
            pltpu.VMEM((length, nv), BF16), pltpu.VMEM((nv, length), BF16), pltpu.VMEM((length, nv), BF16),
            pltpu.VMEM((length, D), BF16), pltpu.VMEM((padded, D), BF16),
            pltpu.VMEM((length, D), BF16), pltpu.VMEM((length, D), BF16), pltpu.VMEM((length, D), BF16),
            pltpu.VMEM((length, D), BF16),
            pltpu.SemaphoreType.DMA((2,)), pltpu.SemaphoreType.DMA((2, count)),
            pltpu.SemaphoreType.DMA((10,)), pltpu.SemaphoreType.DMA((length // BT + 7,)),
        ],
        compiler_params=pltpu.CompilerParams(collective_id=2, has_side_effects=True, vmem_limit_bytes=60 * 2**20),
        name="feed",
    )(tokens, cotangent, attn, recip, wide, gate_turned, down, gains)


def back_kernel(
    pieces, small_pieces, bits, rows,
    pairs_in, values_in, gn_in, gnt_in, gd_in, mask_in, ffn_in, grads_in, normed_in, wide_in, tokens_in,
    total_out, sums_out, grad_out, small_out,
    q_ref, k_ref, v_ref, gn_ref, gnt_ref, gd_ref, mask_ref, normed_ref, wide_ref, tokens_ref,
    part, leaf, mid, total, work, landing, sums, small_work, small_landing, small_sums,
    qt_ref, gq_ref, gkt_ref, gvt_ref, gp_ref, gv_ref, grad_ref, gain_ref,
    line_send, line_recv, cube_send, cube_recv, small_send, small_recv, load_sem, store_sem,
):
    f = lax.axis_index("feat")
    line = LineSum(part, leaf, mid, total, line_send, line_recv, rows, (0, 2, 4))
    cube = CubeSum(work, landing, sums, cube_send, cube_recv, pieces, bits)
    small = CubeSum(small_work, small_landing, small_sums, small_send, small_recv, small_pieces, bits)
    half = HEADS * QK
    first_loads = [
        pltpu.make_async_copy(grads_in.at[pl.ds(a, n)], work.at[pl.ds(a, n)], load_sem.at[m]) for m, (a, n) in enumerate(pieces)
    ] + [pltpu.make_async_copy(ffn_in, part, load_sem.at[len(pieces)])]
    sources = [
        (pairs_in.at[:, pl.ds(0, half)], q_ref), (pairs_in.at[:, pl.ds(half, half)], k_ref), (values_in, v_ref),
        (mask_in, mask_ref), (gn_in, gn_ref), (gd_in, gd_ref), (gnt_in, gnt_ref), (normed_in, normed_ref),
        (wide_in.at[:, pl.ds(0, wide_ref.shape[1])], wide_ref), (tokens_in, tokens_ref),
    ]
    loads = [pltpu.make_async_copy(a, b, load_sem.at[len(pieces) + 1 + n]) for n, (a, b) in enumerate(sources)]
    for load in first_loads:
        load.start()
    greet(line, cube)
    for p in range(len(pieces)):
        first_loads[p].wait()
        cube.launch(p)
    for load in loads[:7]:
        load.start()
    first_loads[-1].wait()
    each(line.leaves, line.count)
    gq_ref[...] = jnp.zeros_like(gq_ref)
    for load in loads[:7]:
        load.wait()
    for load in loads[7:]:
        load.start()
    qt_ref[...] = q_ref[...].T

    lane = lax.broadcasted_iota(jnp.int32, (1, 128), 1)
    length = q_ref.shape[0]
    blocks = length // BT
    hb = 2
    groups = HEADS // hb
    weaver = Weaver(2.0)
    weaver.add("line", line_floors(line, 0.5), [0.0] * line.steps())
    floors, times = cube_floors(cube, 0.0)
    for p in range(len(pieces)):
        weaver.add(("cube", p), floors[p], times[p])

    def take(items):
        for name, n in items:
            if name == "line":
                line.serve(jnp.int32(n))
            elif name[0] == "cube":
                cube.advance(name[1], n)
            else:
                small.advance(name[1], n)

    for block in range(blocks):
        lo = block * BT
        below, there = pl.ds(lo, length - lo), pl.ds(lo, BT)
        plans = [weaver.unit(0.43 * (blocks - block) + 0.1) for _ in range(groups)]

        def group(g, carry):
            h = g * hb
            ql = pl.ds(pl.multiple_of(h // 8 * 128, 128), 128)
            vl = pl.ds(pl.multiple_of(g * 128, 128), 128)
            q, k, v = q_ref[below, ql], k_ref[there, ql], v_ref[there, vl]
            both = jnp.concatenate([gn_ref[below, vl], gd_ref[below, vl]], axis=1)
            mask = mask_ref[block, : length - lo, :]
            gq, turned = None, []
            for a in range(hb):
                km = jnp.where(lane // QK == lax.rem(h + a, 8), k, jnp.zeros_like(k))
                vm = jnp.where(lane // HV == a, v, jnp.zeros_like(v))
                pick = jnp.where(lane == HV * a, jnp.ones_like(v), jnp.zeros_like(v))
                t1 = nt(q, km) + 1.0
                p = (t1 * t1 + 1.0).astype(BF16) * mask
                dp = nt(both, jnp.concatenate([vm, pick], axis=1)).astype(BF16) * mask
                gs = (dp.astype(F32) * t1).astype(BF16)
                out = nn(gs, km)
                gq = out if gq is None else gq + out
                qrows = pl.ds(pl.multiple_of((h + a) * QK, QK), QK)
                vrows = pl.ds(pl.multiple_of((h + a) * HV, HV), HV)
                gkt_ref[qrows, there] = nn(qt_ref[qrows, below], gs)
                turned.append(nn(gnt_ref[vrows, below], p) * 0.5)
            gq_ref[below, ql] += gq
            gvt = jnp.concatenate(turned, axis=0)
            gvt_ref[vl, there] = gvt.astype(BF16)
            gv_ref[there, vl] = gvt.T.astype(BF16)
            for n, plan in enumerate(plans):
                if plan:
                    @pl.when(g == n)
                    def _():
                        take(plan)
            return carry

        lax.fori_loop(0, groups, group, 0)
    gp_ref[:, :half] = (gq_ref[...] * 0.25).astype(BF16)
    gp_ref[:, half:] = gkt_ref[...].T.astype(BF16)
    for load in loads[7:]:
        load.wait()

    pair_cols, value_cols = 2 * half // 4, HEADS * HV // 4
    rest = value_cols + pair_cols

    def open_small(p):
        small.launch(p)
        floors, times = cube_floors(small, 0.0, 1.8)
        weaver.add(("small", p), [0.0] * len(floors[p]), times[p])

    small_work[0:value_cols, :] = nn(
        gvt_ref[pl.ds(pl.multiple_of(f * value_cols, value_cols), value_cols), :], normed_ref[...]
    ).astype(BF16)
    small_work[value_cols:rest, :] = nn(own_column(gp_ref, f, pair_cols).T, normed_ref[...]).astype(BF16)
    if len(small_pieces) > 1:
        open_small(0)
    take(weaver.unit(3.6))
    gain_ref[...] = jnp.zeros_like(gain_ref)
    for n in range(blocks):
        at = slice(n * BT, (n + 1) * BT)
        grad = nt(gp_ref[at, :], wide_ref[:, : 2 * half]) + nt(gv_ref[at, :], wide_ref[:, 2 * half :])
        grad_ref[at, :] = grad.astype(BF16)
        x = tokens_ref[at, :].astype(F32)
        scale = lax.rsqrt(jnp.mean(x * x, axis=1, keepdims=True) + EPS)
        gain_ref[0:1, :] += jnp.sum(grad * (x * scale), axis=0, keepdims=True)
        if n < blocks - 1:
            take(weaver.unit(1.4))
    grad_store = pltpu.make_async_copy(grad_ref, grad_out, store_sem.at[0])
    grad_store.start()
    small_work[rest:, :] = jnp.zeros((small_work.shape[0] - rest, D), BF16)
    small_work[rest : rest + 16, :] = gain_ref[...].astype(BF16)
    open_small(len(small_pieces) - 1)
    take(weaver.unit(1.6))
    take(weaver.until([("cube", p) for p in range(len(pieces))]))
    sums_store = pltpu.make_async_copy(sums, sums_out, store_sem.at[2])
    sums_store.start()
    take(weaver.until([("small", p) for p in range(len(small_pieces))]))
    small_store = pltpu.make_async_copy(small_sums, small_out, store_sem.at[1])
    small_store.start()
    take(weaver.until(["line"]))
    each(line.arrived, line.count)
    total_store = pltpu.make_async_copy(total, total_out, store_sem.at[3])
    total_store.start()
    line.drain()
    cube.drain()
    small.drain()
    for s in (sums_store, grad_store, small_store, total_store):
        s.wait()


def back(pairs, values, gn, gnt, gd, mask, ffn, grads, normed, wide, tokens, pieces, bits, dp_size):
    length = tokens.shape[0]
    nq, nv, rows = HEADS * QK, HEADS * HV, 64
    count = length // rows
    unit = 16 * dp_size
    first = (nv // 4 + nq // 2) // unit * unit
    small_pieces = [(0, first), (first, unit)] if first else []
    small_rows = first + unit
    need = nv // 4 + nq // 2 + 16
    if small_rows < need or not small_pieces:
        small_rows = (need + unit - 1) // unit * unit
        small_pieces = [(0, small_rows)]
    hbm = pl.BlockSpec(memory_space=pl.ANY)

    def buf(*shape, dtype=BF16):
        return pltpu.VMEM(shape, dtype)

    sems = []
    for p in (pieces, small_pieces):
        sems += [pltpu.SemaphoreType.DMA((2,)), pltpu.SemaphoreType.DMA((len(p), 2, 2 * len(bits)))]
    return pl.pallas_call(
        functools.partial(back_kernel, pieces, small_pieces, bits, rows),
        out_shape=(
            jax.ShapeDtypeStruct((length, D), BF16),
            jax.ShapeDtypeStruct(grads.shape, BF16),
            jax.ShapeDtypeStruct((length, D), BF16),
            jax.ShapeDtypeStruct((small_rows, D), BF16),
        ),
        in_specs=[hbm] * 11,
        out_specs=(hbm,) * 4,
        scratch_shapes=[
            buf(length, nq), buf(length, nq), buf(length, nv), buf(length, nv), buf(nv, length), buf(length, nv),
            buf(*mask.shape), buf(length, D), buf(D, 2 * nq + nv), buf(length, D),
            buf(length, D), buf(length, D), buf(length, D), buf(length, D),
            buf(*grads.shape), buf(*grads.shape), buf(*grads.shape),
            buf(small_rows, D), buf(small_rows, D), buf(small_rows, D),
            buf(nq, length), buf(length, nq, dtype=F32), buf(nq, length, dtype=F32), buf(nv, length), buf(length, 2 * nq), buf(length, nv),
            buf(length, D), buf(16, D, dtype=F32),
            pltpu.SemaphoreType.DMA((2,)), pltpu.SemaphoreType.DMA((2, count)), *sems,
            pltpu.SemaphoreType.DMA((len(pieces) + 11,)), pltpu.SemaphoreType.DMA((4,)),
        ],
        compiler_params=pltpu.CompilerParams(collective_id=4, has_side_effects=True, vmem_limit_bytes=62 * 2**20),
        name="back",
    )(pairs, values, gn, gnt, gd, mask, ffn, grads, normed, wide, tokens)


def update_kernel(
    rates,
    down_w, down_m, down_a, gate_w, gate_m, gate_a, out_w, out_m, out_a, value_w, value_m, value_a,
    pair_w, pair_m, pair_a, gain_w, gain_m, gain_a, big, small, hidden, total, grad_hidden, grad_normed, tokens, gains,
    mixed_o, input_o, pair_mo, pair_wo, pair_ao, value_mo, value_wo, value_ao, out_mo, out_wo, out_ao,
    gate_mo, gate_wo, gate_ao, down_mo, down_wo, down_ao, gain_mo, gain_wo, gain_ao,
):
    ff = down_w.shape[0]
    narrow = value_w.shape[1]
    pair_cols = pair_w.shape[1]

    def put(index, outs, grad, w, m, a, rate):
        moment_next, weight_next, average_next = update(w[index], grad, m[index], a[index], rate)
        outs[0][index], outs[1][index], outs[2][index] = moment_next, weight_next, average_next

    put(..., (down_mo, down_wo, down_ao), big[:ff, :].astype(F32), down_w, down_m, down_a, rates[4])
    for n in range(2):
        first = (n + 1) * ff
        put(n, (gate_mo, gate_wo, gate_ao), big[first : first + ff, :].astype(F32), gate_w, gate_m, gate_a, rates[3])
    first = 3 * ff
    put(..., (out_mo, out_wo, out_ao), big[first : first + out_w.shape[0], :].astype(F32), out_w, out_m, out_a, rates[2])
    first = first + out_w.shape[0]
    put(..., (value_mo, value_wo, value_ao), small[:narrow, :].astype(F32).T, value_w, value_m, value_a, rates[1])
    put(..., (pair_mo, pair_wo, pair_ao), small[narrow : narrow + pair_cols, :].astype(F32).T, pair_w, pair_m, pair_a, rates[0])
    gain_one = small[narrow + pair_cols : narrow + pair_cols + 16, :].astype(F32)[0:1, :]
    gain_two = big[first : first + 16, :].astype(F32)[0:1, :]
    put(slice(0, 1), (gain_mo, gain_wo, gain_ao), gain_one, gain_w, gain_m, gain_a, rates[5])
    put(slice(1, 2), (gain_mo, gain_wo, gain_ao), gain_two, gain_w, gain_m, gain_a, rates[5])

    mixed_o[...] = (hidden[...] + total[...].astype(F32)).astype(BF16)
    x = tokens[...].astype(F32)
    scale = lax.rsqrt(jnp.mean(x * x, axis=1, keepdims=True) + EPS)
    unit = x * scale
    u = grad_normed[...].astype(F32) * gains[0:1, :]
    input_o[...] = grad_hidden[...] + scale * (u - unit * jnp.mean(u * unit, axis=1, keepdims=True))


def finish(rates, weights, big, small, hidden, total, grad_hidden, grad_normed, tokens, gains):
    length = tokens.shape[0]
    steps = D // 128
    rows = length // steps
    ff = weights[0][0].shape[0]
    narrow, pair_cols = weights[3][0].shape[1], weights[4][0].shape[1]

    def cols(n):
        return pl.BlockSpec((n, 128), lambda i: (0, i))

    def tall(n):
        return pl.BlockSpec((128, n), lambda i: (i, 0))

    token = pl.BlockSpec((rows, D), lambda i: (i, 0))
    specs = [cols(ff), pl.BlockSpec((2, ff, 128), lambda i: (0, 0, i)), cols(weights[2][0].shape[0]), tall(narrow), tall(pair_cols), cols(2)]
    order = [4, 3, 2, 1, 0, 5]
    flat = [a for group in weights for a in group]
    out_shape = [jax.ShapeDtypeStruct((length, D), BF16), jax.ShapeDtypeStruct((length, D), F32)]
    out_specs = [token, token]
    for n in order:
        out_shape += [jax.ShapeDtypeStruct(weights[n][0].shape, F32)] * 3
        out_specs += [specs[n]] * 3
    in_specs = [specs[n] for n in range(6) for _ in range(3)]
    in_specs += [cols(big.shape[0]), cols(small.shape[0])] + [token] * 5 + [pl.BlockSpec((2, D), lambda i: (0, 0))]
    return pl.pallas_call(
        functools.partial(update_kernel, rates),
        grid=(steps,),
        out_shape=out_shape,
        in_specs=in_specs,
        out_specs=out_specs,
        compiler_params=pltpu.CompilerParams(vmem_limit_bytes=62 * 2**20),
        name="finish",
    )(*flat, big, small, hidden, total, grad_hidden, grad_normed, tokens, gains)


def update(weight, grad_total, moment, average, rate):
    moment_next = MOMENTUM * moment + grad_total
    weight_next = weight - rate * (grad_total + MOMENTUM * moment_next)
    average_next = average + (weight_next - average) / STEP
    return (moment_next, weight_next, average_next)


def on_device(
    tokens,
    cotangent,
    doc_starts,
    queries_keys,
    value_weight,
    out_weight,
    gate_up,
    down_weight,
    norm_gains,
    queries_moment,
    value_moment,
    out_moment,
    gate_moment,
    down_moment,
    gains_moment,
    queries_average,
    value_average,
    out_average,
    gate_average,
    down_average,
    gains_average,
):
    total_tokens = float(tokens.shape[0] * lax.axis_size("dp"))
    dp_size = lax.axis_size("dp")
    ff = down_weight.shape[0]
    gate_turned = gate_up.transpose(0, 2, 1)
    normed_one, pairs, values, wide, gate_low, down_low, attn_low, recip, mask = front(
        doc_starts, tokens, norm_gains, queries_keys, value_weight, out_weight, gate_turned, down_weight
    )
    padded, pieces, bits = cube_shape(3 * ff + out_weight.shape[0] + 16, dp_size, 4)
    hidden_one, grad_hidden, grad_numer, grad_numer_turned, grad_denom, ffn_part, big = feed(
        tokens, cotangent, attn_low, recip, wide, gate_low, down_low, norm_gains, padded
    )
    total, big, grad_normed_one, small = back(
        pairs, values, grad_numer, grad_numer_turned, grad_denom, mask, ffn_part, big, normed_one, wide, tokens,
        pieces, bits, dp_size,
    )
    rates = (
        (D * total_tokens) ** (-0.5),
        (D * total_tokens) ** (-0.5),
        (HEADS * HV * total_tokens) ** (-0.5),
        (D * total_tokens) ** (-0.5),
        (FF * total_tokens) ** (-0.5),
        0.2 * total_tokens ** (-0.5),
    )
    weights = (
        (down_weight, down_moment, down_average),
        (gate_turned, gate_moment.transpose(0, 2, 1), gate_average.transpose(0, 2, 1)),
        (out_weight, out_moment, out_average),
        (value_weight, value_moment, value_average),
        (queries_keys, queries_moment, queries_average),
        (norm_gains, gains_moment, gains_average),
    )
    outs = list(finish(rates, weights, big, small, hidden_one, total, grad_hidden, grad_normed_one, tokens, norm_gains))
    outs[11:14] = [o.transpose(0, 2, 1) for o in outs[11:14]]
    return tuple(outs)


def solution(mesh):
    in_specs = (
        P("dp", None),
        P("dp", None),
        P("dp", None),
        P(None, "feat"),
        P(None, "feat"),
        P("feat", None),
        P(None, None, "feat"),
        P("feat", None),
        P(),
        P(None, "feat"),
        P(None, "feat"),
        P("feat", None),
        P(None, None, "feat"),
        P("feat", None),
        P(),
        P(None, "feat"),
        P(None, "feat"),
        P("feat", None),
        P(None, None, "feat"),
        P("feat", None),
        P(),
    )
    out_specs = (
        P("dp", None),
        P("dp", None),
        P(None, "feat"),
        P(None, "feat"),
        P(None, "feat"),
        P(None, "feat"),
        P(None, "feat"),
        P(None, "feat"),
        P("feat", None),
        P("feat", None),
        P("feat", None),
        P(None, None, "feat"),
        P(None, None, "feat"),
        P(None, None, "feat"),
        P("feat", None),
        P("feat", None),
        P("feat", None),
        P(),
        P(),
        P(),
    )
    return jax.shard_map(
        on_device, mesh=mesh, in_specs=in_specs, out_specs=out_specs, check_vma=False
    )
```

profile of v0, /device:TPU:0, one launch (start us, length us, event | category | flops | bytes accessed | tf_op | source)
XLA Modules:
  0.0 224.0 jit_solution(10555181304192871397)
XLA Ops:
  0.7 47.2 %front.1 = (bf16[1024,1024]{1,0:T(8,128)(2,1)}, bf16[1024,512]{1,0:T(8,128)(2,1)}, bf16[1024,1024]{1,0:T(8,128)(2,1)}, bf16[1024,2560]{1,0:T(8,128)(2,1)}, bf16[...) custom-call(s32[1,8]{1,0:T(1,128)} %starts_ref.1, ...), custom_call_target="tpu_custom_call" | custom-call | tf_op jit(solution)/shard_map/front/pallas_call | solution.py:616
  47.8 71.3 %feed.1 = (f32[1024,1024]{1,0:T(8,128)}, f32[1024,1024]{1,0:T(8,128)}, bf16[1024,1024]{1,0:T(8,128)(2,1)}, bf16[1024,1024]{1,0:T(8,128)(2,1)}, bf16[1024,1024]{1...) custom-call(bf16[1024,1024]{1,0:T(8,128)(2,1)} %tokens.1, bf16[1024,1024]{1,0:T(8,128)(2,1)} %cot_in.1, ...), custom_call_target="tpu_custom_call" | custom-call | tf_op jit(solution)/shard_map/feed/pallas_call | solution.py:820
  119.2 71.5 %back.1 = (bf16[1024,1024]{1,0:T(8,128)(2,1)}, bf16[2432,1024]{1,0:T(8,128)(2,1)}, bf16[1024,1024]{1,0:T(8,128)(2,1)}, bf16[512,1024]{1,0:T(8,128)(2,1)}) custom-call(bf16[1024,512]{1,0:T(8,128)(2,1)} %get-tuple-element.60.pairs_in, bf16[1024,1024]{1,0:T(8,128)(2,1)} %get-tuple-element.61.values_in, bf16[1024,1024]{1,0:T(8,128)(2,1)} %get-tuple-element.67.gn_in, ...), custom_call_target="tpu_custom_call" | custom-call | tf_op jit(solution)/shard_map/back/pallas_call | solution.py:1023
  190.6 33.2 %finish.1 = (bf16[1024,1024]{1,0:T(8,128)(2,1)}, f32[1024,1024]{1,0:T(8,128)}, f32[1024,128]{1,0:T(8,128)}, f32[1024,128]{1,0:T(8,128)}, f32[1024,128]{1,0:T(8,1...) custom-call(f32[688,1024]{1,0:T(8,128)} %down_w.1, ...), custom_call_target="tpu_custom_call" | custom-call | tf_op jit(solution)/shard_map/finish/pallas_call | solution.py:1110
where the time goes:
time: 226 us; the launch traced here: 224 us
  Pallas kernels  223 us (99%)
    pallas_call x1, Pallas kernels, back(): pl.pallas_call(functools.partial(back_kernel, pieces, small_pieces, bits,...  71.5 us
    pallas_call x1, Pallas kernels, feed(): pl.pallas_call(functools.partial(feed_kernel, rows), out_shape=(jax.Shape...  71.3 us
    pallas_call x1, Pallas kernels, front(): pl.pallas_call(functools.partial(front_kernel, bits), out_shape=tuple((ja...  47.2 us
    pallas_call x1, Pallas kernels, finish(): pl.pallas_call(functools.partial(update_kernel, rates), grid=(steps,), ou...  33.2 us

commit v1 on v0

--- a/solution.py
+++ b/solution.py
@@ -255,7 +255,7 @@
 
 
 class Weaver:
-    def __init__(self, now, margin=0.5, cost=0.35):
+    def __init__(self, now, margin=0.5, cost=0.25):
         self.now, self.margin, self.cost = now, margin, cost
         self.streams = {}
 

time: 226 us -> 226 us (level)
  no operation moved by 1% of the time
where the time goes in v1:
time: 226 us; the launch traced here: 223 us
  Pallas kernels  223 us (99%)
    pallas_call x1, Pallas kernels, feed(): pl.pallas_call(functools.partial(feed_kernel, rows), out_shape=(jax.Shape...  71.3 us
    pallas_call x1, Pallas kernels, back(): pl.pallas_call(functools.partial(back_kernel, pieces, small_pieces, bits,...  70.9 us
    pallas_call x1, Pallas kernels, front(): pl.pallas_call(functools.partial(front_kernel, bits), out_shape=tuple((ja...  47.2 us
    pallas_call x1, Pallas kernels, finish(): pl.pallas_call(functools.partial(update_kernel, rates), grid=(steps,), ou...  33.2 us

profile of v1, /device:TPU:0, one launch (start us, length us, event | category | flops | bytes accessed | tf_op | source)
XLA Modules:
  0.0 223.5 jit_solution(3946839879441328026)
XLA Ops:
  0.7 47.2 %front.1 = (bf16[1024,1024]{1,0:T(8,128)(2,1)}, bf16[1024,512]{1,0:T(8,128)(2,1)}, bf16[1024,1024]{1,0:T(8,128)(2,1)}, bf16[1024,2560]{1,0:T(8,128)(2,1)}, bf16[...) custom-call(s32[1,8]{1,0:T(1,128)} %starts_ref.1, ...), custom_call_target="tpu_custom_call" | custom-call | tf_op jit(solution)/shard_map/front/pallas_call | solution.py:616
  47.8 71.3 %feed.1 = (f32[1024,1024]{1,0:T(8,128)}, f32[1024,1024]{1,0:T(8,128)}, bf16[1024,1024]{1,0:T(8,128)(2,1)}, bf16[1024,1024]{1,0:T(8,128)(2,1)}, bf16[1024,1024]{1...) custom-call(bf16[1024,1024]{1,0:T(8,128)(2,1)} %tokens.1, bf16[1024,1024]{1,0:T(8,128)(2,1)} %cot_in.1, ...), custom_call_target="tpu_custom_call" | custom-call | tf_op jit(solution)/shard_map/feed/pallas_call | solution.py:820
  119.2 70.9 %back.1 = (bf16[1024,1024]{1,0:T(8,128)(2,1)}, bf16[2432,1024]{1,0:T(8,128)(2,1)}, bf16[1024,1024]{1,0:T(8,128)(2,1)}, bf16[512,1024]{1,0:T(8,128)(2,1)}) custom-call(bf16[1024,512]{1,0:T(8,128)(2,1)} %get-tuple-element.60.pairs_in, bf16[1024,1024]{1,0:T(8,128)(2,1)} %get-tuple-element.61.values_in, bf16[1024,1024]{1,0:T(8,128)(2,1)} %get-tuple-element.67.gn_in, ...), custom_call_target="tpu_custom_call" | custom-call | tf_op jit(solution)/shard_map/back/pallas_call | solution.py:1023
  190.1 33.2 %finish.1 = (bf16[1024,1024]{1,0:T(8,128)(2,1)}, f32[1024,1024]{1,0:T(8,128)}, f32[1024,128]{1,0:T(8,128)}, f32[1024,128]{1,0:T(8,128)}, f32[1024,128]{1,0:T(8,1...) custom-call(f32[688,1024]{1,0:T(8,128)} %down_w.1, ...), custom_call_target="tpu_custom_call" | custom-call | tf_op jit(solution)/shard_map/finish/pallas_call | solution.py:1110
